TPU v7x, 128 devices: a whole 4x4x4 slice. The times are simulated.
128 devices in a mesh: gen: 8 (over y_hi, x), dom: 8 (over z, y_lo), dp: 2 (over core).
Axes of the slice: x: 4, y: 4 (y_hi: 2, y_lo: 2; y = y_hi * 2 + y_lo), z: 4, core: 2. Of those that a mesh axis runs over, the one named last changes fastest.
Arguments:
- gen_hidden: bfloat16 [2048, 4096], P(('dp', 'dom'), 'gen'), parts along dimension 0, may hold values from -52 to 52
- gen_gain: float32 [8192], P('dp'), parts along dimension 0, may hold values from 0.25 to 1.75
- gen_head: bfloat16 [131072, 4096], P(('dp', 'gen', 'dom')), parts along dimension 0, may hold values from -24 to 24
- dom_hidden: bfloat16 [2048, 4096], P(('dp', 'gen'), 'dom'), parts along dimension 0, may hold values from -52 to 52
- dom_gain: float32 [8192], P('dp'), parts along dimension 0, may hold values from 0.25 to 1.75
- dom_head: bfloat16 [131072, 4096], P(('dp', 'gen', 'dom')), parts along dimension 0, may hold values from -24 to 24
- targets: int32 [2048], P('dp'), parts along dimension 0, may hold values from 0 to 65535
- doc_ids: int32 [2048], P('dp'), parts along dimension 0, may hold values from -1 to 63, as said below
Outputs:
- token_diff: float32 [2048], P(('dp', 'dom')), parts along dimension 0
- doc_score: float32 [128], P(('dp', 'dom')), parts along dimension 0
There are 2 independent parts, one for each index of `dp`. A program takes and returns all parts, laid end to end along the dimension named above; each array names one. Nothing has to cross between parts.
Inputs may be any that keep to these rules, and one draw needn't show every extreme that they name: `doc_ids`: rows 128 * p to 128 * p + 127 form pack p. Each pack begins with rows of exactly 8 documents, numbered 8 * p onwards in order, each one row or more, and ends with padding rows marked -1. The packs fall into pairs whose document rows add up to 136, so the batch holds 544 document rows, and some pack has no padding.
All inputs are finite; a program needn't handle non-finite values.
Results may differ from a plain program's by a relative error of at most 0.0045.
Values may be sent and summed in bfloat16 or wider, within the bound.
A program may use at most 128 MiB of HBM per device.

v0:
```python
import jax
import jax.numpy as jnp
from jax import lax
from jax.sharding import PartitionSpec as P

DOC_PACK = 8


def joined(shard, axis, combine):
    everything = jax.tree.map(lambda part: lax.all_gather(part, axis), shard)
    first = jax.tree.map(lambda part: part[0], everything)

    def turn(k, so_far):
        return combine(so_far, jax.tree.map(lambda part: part[k], everything))

    return lax.fori_loop(1, lax.axis_size(axis), turn, first)


def scale_rows(values_bf, scaling, sum_axes, full_width):
    values = values_bf.astype(jnp.float32)
    meansq = jnp.sum(values * values, axis=sum_axes, keepdims=True) / full_width
    return (values * lax.rsqrt(meansq + 1e-05) * scaling).astype(jnp.bfloat16)


def row_stats(logits, wanted):
    highest = jnp.max(logits, axis=1)
    exp_total = jnp.sum(jnp.exp(logits - highest[:, None]), axis=1)
    columns = lax.broadcasted_iota(jnp.int32, logits.shape, 1)
    picked = jnp.sum(jnp.where(columns == wanted[:, None], logits, 0.0), axis=1)
    return (highest, exp_total, picked)


def combine(former, latter):
    highest = jnp.maximum(former[0], latter[0])
    exp_total = former[1] * jnp.exp(former[0] - highest) + latter[1] * jnp.exp(latter[0] - highest)
    return (highest, exp_total, former[2] + latter[2])


def general_stats(gen_hidden, gen_gain, gen_head, wanted_all):
    rows_dev, width_dev = gen_hidden.shape
    full_width = gen_gain.shape[0]
    gen_count = lax.axis_size("gen")
    dom_count = lax.axis_size("dom")
    block_rows = gen_head.shape[0]
    rows_all = rows_dev * dom_count
    blocks = lax.all_gather(gen_hidden[None], ("gen", "dom"), axis=0, tiled=True)
    blocks = blocks.reshape(gen_count, rows_all, width_dev)
    gain_blocks = gen_gain.reshape(gen_count, 1, width_dev)
    head_blocks = gen_head.reshape(block_rows, gen_count, width_dev)
    normed = scale_rows(blocks, gain_blocks, (0, 2), full_width)
    logits = lax.dot_general(
        normed, head_blocks, (((0, 2), (1, 2)), ((), ())), preferred_element_type=jnp.float32
    )
    row_totals = row_stats(logits, wanted_all)
    highest, exp_total, picked = joined(row_totals, ("gen", "dom"), combine)
    return picked - (highest + jnp.log(exp_total))


def domain_stats(dom_hidden, dom_gain, dom_head, wanted_all):
    rows_dev, width_dev = dom_hidden.shape
    full_width = dom_gain.shape[0]
    gen_count = lax.axis_size("gen")
    dom_count = lax.axis_size("dom")
    block_rows = dom_head.shape[0]
    rows_all = rows_dev * gen_count
    blocks = lax.all_gather(dom_hidden[None], ("gen", "dom"), axis=0, tiled=True)
    blocks = blocks.reshape(gen_count, dom_count, rows_dev, width_dev)
    head_blocks = dom_head.reshape(block_rows, dom_count, width_dev)
    gain_blocks = dom_gain.reshape(1, dom_count, 1, width_dev)
    normed = scale_rows(blocks, gain_blocks, (1, 3), full_width)
    logits = lax.dot_general(
        normed, head_blocks, (((1, 3), (1, 2)), ((), ())), preferred_element_type=jnp.float32
    )
    row_totals = row_stats(logits.reshape(rows_all, block_rows), wanted_all)
    highest, exp_total, picked = joined(row_totals, ("gen", "dom"), combine)
    return picked - (highest + jnp.log(exp_total))


def per_device(gen_hidden, gen_gain, gen_head, dom_hidden, dom_gain, dom_head, targets, doc_ids):
    rows_dev = gen_hidden.shape[0]
    first_column = (
        lax.axis_index("gen") * lax.axis_size("dom") + lax.axis_index("dom")
    ) * gen_head.shape[0]
    wanted_all = targets - first_column
    gen_logprob = general_stats(gen_hidden, gen_gain, gen_head, wanted_all)
    dom_logprob = domain_stats(dom_hidden, dom_gain, dom_head, wanted_all)
    is_live = doc_ids >= 0
    token_all = jnp.where(is_live, dom_logprob - gen_logprob, 0.0)
    pack_index = lax.axis_index("dom")
    token_own = lax.dynamic_slice_in_dim(token_all, pack_index * rows_dev, rows_dev)
    docs_own = (
        lax.dynamic_slice_in_dim(doc_ids, pack_index * rows_dev, rows_dev) - pack_index * DOC_PACK
    )
    onehot = (docs_own[:, None] == jnp.arange(DOC_PACK, dtype=jnp.int32)[None, :]).astype(
        jnp.float32
    )
    doc_sums = jnp.dot(token_own, onehot, precision=lax.Precision.HIGHEST)
    counts = jnp.sum(onehot, axis=0)
    return (token_own, doc_sums / counts)


def solution(mesh):
    in_specs = (
        P(("dp", "dom"), "gen"),
        P("dp"),
        P(("dp", "gen", "dom"), None),
        P(("dp", "gen"), "dom"),
        P("dp"),
        P(("dp", "gen", "dom"), None),
        P("dp"),
        P("dp"),
    )
    out_specs = (P(("dp", "dom")), P(("dp", "dom")))
    return jax.shard_map(
        per_device, mesh=mesh, in_specs=in_specs, out_specs=out_specs, check_vma=False
    )
```

profile of v0, /device:TPU:8, one launch (start us, length us, event | category | flops | bytes accessed | tf_op | source)
XLA Modules:
  0.0 1784.5 jit_solution(5406152321257120198)
XLA Ops:
  7.2 0.0 all-gather.11.cloned.1.call-start
  7.2 0.7 all-gather.11.cloned.1.call-update
  7.9 0.0 all-gather.13.cloned.1.call-start
  7.9 0.7 all-gather.13.cloned.1.call-update
  8.7 0.7 mul.110
  9.4 0.7 mul.120
  10.1 0.8 dynamic-slice_subtract_fusion
  10.9 0.1 convert_reduce_fusion
  11.0 0.7 broadcast_subtract_fusion
  11.7 340.2 %all-gather.11.cloned.1.call-done = bf16[8192,512]{1,0:T(8,128)(2,1)} async-done(((bf16[128,512]{1,0:T(8,128)(2,1)}), bf16[8192,512]{1,0:T(8,128)(2,1)}) %all-gather.11.cloned.1.call-update) | async-done | bytes 8388624 | tf_op jit(solution)/shard_map/all_gather | solution.py:66
  351.9 5.1 multiply_reduce_fusion
  357.1 9.4 fusion.3
  366.4 7.6 copy.16
  374.0 321.7 %all-gather.13.cloned.1.call-done = bf16[8192,512]{1,0:T(8,128)(2,1)} async-done(((bf16[128,512]{1,0:T(8,128)(2,1)}), bf16[8192,512]{1,0:T(8,128)(2,1)}) %all-gather.13.cloned.1.call-update) | async-done | bytes 8388624 | tf_op jit(solution)/shard_map/all_gather | solution.py:46
  695.7 5.1 fusion
  700.9 0.0 copy-start
  700.9 13.2 bitcast_reduce_fusion.1
  714.1 0.0 copy-done
  714.2 2.5 fusion.2
  716.6 11.3 bitcast_reduce_fusion
  727.9 0.0 copy-start.1
  727.9 2.0 fusion.15
  729.9 173.9 %all-gather.2 = f32[65536]{0:T(1024)S(1)} all-gather(f32[1024]{0:T(1024)S(1)} %get-tuple-element.365), channel_id=4, replica_groups=mesh['gen'=8,'dom'=8,'dp'=2] {'gen','dom'}, dimensions={0}, use_global_device_ids=true | all-gather | bytes 266240 | tf_op jit(solution)/shard_map/all_gather | solution.py:10
  903.9 174.6 %all-gather.3 = f32[65536]{0:T(1024)S(1)} all-gather(f32[1024]{0:T(1024)S(1)} %get-tuple-element.364), channel_id=5, replica_groups=mesh['gen'=8,'dom'=8,'dp'=2] {'gen','dom'}, dimensions={0}, use_global_device_ids=true | all-gather | bytes 266240 | tf_op jit(solution)/shard_map/all_gather | solution.py:10
  1078.6 170.6 %all-gather.1 = f32[65536]{0:T(1024)S(1)} all-gather(f32[1024]{0:T(1024)S(1)} %get-tuple-element.408), channel_id=3, replica_groups=mesh['gen'=8,'dom'=8,'dp'=2] {'gen','dom'}, dimensions={0}, use_global_device_ids=true | all-gather | bytes 266240 | tf_op jit(solution)/shard_map/all_gather | solution.py:10
  1249.3 172.5 %all-gather.6 = f32[65536]{0:T(1024)S(1)} all-gather(f32[1024]{0:T(1024)S(1)} %get-tuple-element.368), channel_id=8, replica_groups=mesh['gen'=8,'dom'=8,'dp'=2] {'gen','dom'}, dimensions={0}, use_global_device_ids=true | all-gather | bytes 266240 | tf_op jit(solution)/shard_map/all_gather | solution.py:10
  1421.8 170.6 %all-gather.7 = f32[65536]{0:T(1024)S(1)} all-gather(f32[1024]{0:T(1024)S(1)} %get-tuple-element.369), channel_id=9, replica_groups=mesh['gen'=8,'dom'=8,'dp'=2] {'gen','dom'}, dimensions={0}, use_global_device_ids=true | all-gather | bytes 266240 | tf_op jit(solution)/shard_map/all_gather | solution.py:10
  1592.5 172.5 %all-gather.5 = f32[65536]{0:T(1024)S(1)} all-gather(f32[1024]{0:T(1024)S(1)} %get-tuple-element.406), channel_id=7, replica_groups=mesh['gen'=8,'dom'=8,'dp'=2] {'gen','dom'}, dimensions={0}, use_global_device_ids=true | all-gather | bytes 266240 | tf_op jit(solution)/shard_map/all_gather | solution.py:10
  1765.1 5.9 while.38
  1771.0 5.9 while.39
  1776.9 0.1 dynamic_slice.66
  1777.0 0.6 fusion.16
  (527 shorter events, 6.0 us)
Async XLA Ops:
  7.2 344.8 %all-gather.11.cloned.1.call-start = ((), (), s32[]{:S(2)}) async-start(), calls=%async_computation | async-start | bytes 8519680 | tf_op jit(solution)/shard_map/all_gather | solution.py:66
  7.9 687.8 %all-gather.13.cloned.1.call-start = ((), (), s32[]{:S(2)}) async-start(), calls=%async_computation.1 | async-start | bytes 8519680 | tf_op jit(solution)/shard_map/all_gather | solution.py:46
  700.9 13.2 copy-start
  727.9 1049.0 %copy-start.1 = (s32[1024]{0:T(1024)S(1)}, s32[1024]{0:T(1024)}, u32[]{:S(2)}) copy-start(s32[1024]{0:T(1024)} %param.19) | copy-start | bytes 12292
  1777.0 0.6 copy-start.2
Sparse Core Ops, SparseCore 0:
  9.6 342.2 all-gather.10
  353.6 342.1 all-gather.12
where the time goes:
time: 1780 us
  blocking collectives  1030 us (58%)
  waiting for transfers between devices  663 us (37%)
  other arithmetic  27.7 us (2%)
  matrix products  25.1 us (1%)
    all_gather x6, blocking collectives, joined(): everything = jax.tree.map(lambda part: lax.all_gather(part, axis), shard)  1030 us
    all_gather x1, waiting for transfers between devices, domain_stats(): lax.all_gather(dom_hidden[None], ('gen', 'dom'), axis=0, tiled=True)  340 us
    all_gather x1, waiting for transfers between devices, general_stats(): lax.all_gather(gen_hidden[None], ('gen', 'dom'), axis=0, tiled=True)  322 us
  transfers between devices with their start and end apart: 2, of which 2 were waited for; matrix products, arithmetic and copies ran while one was open for 1% of the time, Pallas kernels for 0%

commit v1 on v0

--- a/solution.py
+++ b/solution.py
@@ -43,7 +43,11 @@
     dom_count = lax.axis_size("dom")
     block_rows = gen_head.shape[0]
     rows_all = rows_dev * dom_count
-    blocks = lax.all_gather(gen_hidden[None], ("gen", "dom"), axis=0, tiled=True)
+    part_2 = gen_hidden[None]
+    size = lax.axis_size(("gen", "dom"))
+    pieces = jnp.stack([part_2 for _ in range(size)])
+    pieces = lax.all_to_all(pieces, ("gen", "dom"), split_axis=0, concat_axis=0)
+    blocks = jnp.concatenate(pieces, axis=0)
     blocks = blocks.reshape(gen_count, rows_all, width_dev)
     gain_blocks = gen_gain.reshape(gen_count, 1, width_dev)
     head_blocks = gen_head.reshape(block_rows, gen_count, width_dev)

time: 1780 us -> 1370 us (0.77)
  waiting for transfers between devices: 663 us -> 226 us
    all_gather x1 -> x0, waiting for transfers between devices: 322 us -> none  [general_stats(): lax.all_gather(gen_hidden[None], ('gen', 'dom'), axis=0, tiled=True)]
    all_gather x1, waiting for transfers between devices: 340 us -> 93.6 us  [domain_stats(): lax.all_gather(dom_hidden[None], ('gen', 'dom'), axis=0, tiled=True)]
    all_to_all x0 -> x1, waiting for transfers between devices: none -> 132 us  [general_stats(): pieces = lax.all_to_all(pieces, ('gen', 'dom'), split_axis=0, concat_axis=0)]
  transfers between devices with their start and end apart: 2 -> 2, of which waited for: 2 -> 2; matrix products, arithmetic and copies ran while one was open for 1% -> 2% of each run, Pallas kernels for 0% -> 0%
where the time goes in v1:
time: 1370 us
  blocking collectives  1030 us (75%)
  waiting for transfers between devices  226 us (16%)
  other arithmetic  29.2 us (2%)
  matrix products  26.2 us (2%)
  local copies, waits for them, and re-layouts  16.8 us (1%)
  between operations  14.3 us (1%)
    all_gather x6, blocking collectives, joined(): everything = jax.tree.map(lambda part: lax.all_gather(part, axis), shard)  1030 us
    all_to_all x1, waiting for transfers between devices, general_stats(): pieces = lax.all_to_all(pieces, ('gen', 'dom'), split_axis=0, concat_axis=0)  132 us
    all_gather x1, waiting for transfers between devices, domain_stats(): lax.all_gather(dom_hidden[None], ('gen', 'dom'), axis=0, tiled=True)  93.6 us
  transfers between devices with their start and end apart: 2, of which 2 were waited for; matrix products, arithmetic and copies ran while one was open for 2% of the time, Pallas kernels for 0%

profile of v1, /device:TPU:8, one launch (start us, length us, event | category | flops | bytes accessed | tf_op | source)
XLA Modules:
  0.0 1365.1 jit_solution(7607980228907119046)
XLA Ops:
  7.2 0.0 all-gather.9.cloned.1.call-start
  7.2 0.7 all-gather.9.cloned.1.call-update
  7.9 5.1 stack.3
  13.0 11.7 all-to-all-start
  24.8 0.0 copy-done.2
  24.8 0.0 copy-done.3
  24.9 0.0 copy-done.4
  24.9 0.1 dynamic-slice_subtract_fusion
  24.9 0.1 convert_reduce_fusion
  25.1 0.0 copy-done.5
  25.1 131.8 %all-to-all-done = bf16[64,1,128,512]{3,2,1,0:T(8,128)(2,1)} async-done(((bf16[64,1,128,512]{3,2,1,0:T(8,128)(2,1)}), bf16[64,1,128,512]{3,2,1,0:T(8,128)(2,1)}, u32[]{:S(2)}, u32[]{:S(2)}) %all-to-all-start) | async-done | bytes 8388640 | tf_op jit(solution)/shard_map/all_to_all | solution.py:49
  156.9 5.1 fusion
  162.1 5.3 fusion.2
  167.4 12.6 bitcast_reduce_fusion
  180.0 172.3 %all-gather.4 = f32[65536]{0:T(1024)S(1)} all-gather(f32[1024]{0:T(1024)S(1)} %get-tuple-element.406), channel_id=6, replica_groups=mesh['gen'=8,'dom'=8,'dp'=2] {'gen','dom'}, dimensions={0}, use_global_device_ids=true | all-gather | bytes 266240 | tf_op jit(solution)/shard_map/all_gather | solution.py:10
  352.3 93.6 %all-gather.9.cloned.1.call-done = bf16[8192,512]{1,0:T(8,128)(2,1)} async-done(((bf16[128,512]{1,0:T(8,128)(2,1)}), bf16[8192,512]{1,0:T(8,128)(2,1)}) %all-gather.9.cloned.1.call-update) | async-done | bytes 8388624 | tf_op jit(solution)/shard_map/all_gather | solution.py:70
  445.9 5.1 multiply_reduce_fusion
  451.1 9.4 fusion.3
  460.4 7.6 copy.16
  468.0 13.0 bitcast_reduce_fusion.1
  481.0 0.0 slice-start
  481.1 2.0 fusion.15
  483.1 174.1 %all-gather.2 = f32[65536]{0:T(1024)S(1)} all-gather(f32[1024]{0:T(1024)S(1)} %get-tuple-element.365), channel_id=4, replica_groups=mesh['gen'=8,'dom'=8,'dp'=2] {'gen','dom'}, dimensions={0}, use_global_device_ids=true | all-gather | bytes 266240 | tf_op jit(solution)/shard_map/all_gather | solution.py:10
  657.2 174.5 %all-gather.3 = f32[65536]{0:T(1024)S(1)} all-gather(f32[1024]{0:T(1024)S(1)} %get-tuple-element.364), channel_id=5, replica_groups=mesh['gen'=8,'dom'=8,'dp'=2] {'gen','dom'}, dimensions={0}, use_global_device_ids=true | all-gather | bytes 266240 | tf_op jit(solution)/shard_map/all_gather | solution.py:10
  831.7 170.6 %all-gather.1 = f32[65536]{0:T(1024)S(1)} all-gather(f32[1024]{0:T(1024)S(1)} %get-tuple-element.408), channel_id=3, replica_groups=mesh['gen'=8,'dom'=8,'dp'=2] {'gen','dom'}, dimensions={0}, use_global_device_ids=true | all-gather | bytes 266240 | tf_op jit(solution)/shard_map/all_gather | solution.py:10
  1002.4 172.6 %all-gather.5 = f32[65536]{0:T(1024)S(1)} all-gather(f32[1024]{0:T(1024)S(1)} %get-tuple-element.368), channel_id=7, replica_groups=mesh['gen'=8,'dom'=8,'dp'=2] {'gen','dom'}, dimensions={0}, use_global_device_ids=true | all-gather | bytes 266240 | tf_op jit(solution)/shard_map/all_gather | solution.py:10
  1175.0 170.6 %all-gather.6 = f32[65536]{0:T(1024)S(1)} all-gather(f32[1024]{0:T(1024)S(1)} %get-tuple-element.369), channel_id=8, replica_groups=mesh['gen'=8,'dom'=8,'dp'=2] {'gen','dom'}, dimensions={0}, use_global_device_ids=true | all-gather | bytes 266240 | tf_op jit(solution)/shard_map/all_gather | solution.py:10
  1345.7 5.9 while.38
  1351.6 5.9 while.39
  1357.5 0.1 dynamic_slice.66
  1357.6 0.6 fusion.16
  1358.2 0.0 copy-done.6
  (536 shorter events, 6.0 us)
Async XLA Ops:
  7.2 438.8 %all-gather.9.cloned.1.call-start = ((), (), s32[]{:S(2)}) async-start(), calls=%async_computation.1 | async-start | bytes 8519680 | tf_op jit(solution)/shard_map/all_gather | solution.py:70
  13.0 11.8 copy-start.2
  13.0 11.8 copy-start.3
  13.0 11.8 copy-start.4
  13.0 12.0 copy-start.5
  13.0 143.9 %all-to-all-start = ((bf16[64,1,128,512]{3,2,1,0:T(8,128)(2,1)}), bf16[64,1,128,512]{3,2,1,0:T(8,128)(2,1)}, u32[]{:S(2)}, u32[]{:S(2)}) async-start(bf16[64,1,128,512]{3,2,1,0:T(8,128)(2,1)} %stack.3), calls=%async_computation | async-start | bytes 16777216 | tf_op jit(solution)/shard_map/all_to_all | solution.py:49
  352.3 108.1 %copy-start.1 = (f32[65536]{0:T(1024)}, f32[65536]{0:T(1024)S(1)}, u32[]{:S(2)}) copy-start(f32[65536]{0:T(1024)S(1)} %all-gather.4) | copy-start | bytes 786436
  468.0 13.0 copy-start
  481.0 870.5 %slice-start = ((f32[65536]{0:T(1024)}), f32[1024]{0:T(1024)S(1)}, s32[]{:S(2)}) async-start(f32[65536]{0:T(1024)} %copy-done.1), calls=%async_computation.2 | async-start | bytes 8192 | tf_op jit(solution)/shard_map/slice | solution.py:11
  1357.6 0.6 copy-start.6
Sparse Core Ops, SparseCore 0:
  9.6 436.2 all-gather.8
